TPU v7x, 32 devices: a whole 2x2x4 slice. The times are simulated.
32 devices in a mesh: pb: 2 (over y), ka: 4 (over x, core), ha: 4 (over z).
Axes of the slice: x: 2, y: 2, z: 4, core: 2. Of those that a mesh axis runs over, the one named last changes fastest.
Arguments:
- queries: bfloat16 [768, 4096], P(('pb', 'ka'), 'ha'), may hold values from -200 to 200
- latents: bfloat16 [768, 8, 128], P(('ka', 'pb'), 'ha'), may hold values from -6 to 6
- key_up: bfloat16 [8, 64, 128], P('ha'), may hold values from -1.5 to 1.5
- value_up: bfloat16 [8, 64, 128], P('ha'), may hold values from -0.75 to 0.75
- documents: int32 [768], replicated, may hold values from 0 to 3, as said below
Outputs:
- attended: bfloat16 [768, 4096], P(('pb', 'ka'), 'ha')
Inputs may be any that keep to these rules, and one draw needn't show every extreme that they name: `documents`: ids never fall along the prompt; one document holds exactly 384 positions and none holds more.
All inputs are finite; a program needn't handle non-finite values.
Results may differ from a plain program's by a relative error of at most 0.009.
Values may be sent and summed in bfloat16 or wider, within the bound.
A program may use at most 128 MiB of HBM per device.

v0:
```python
import functools
import math

import jax
import jax.numpy as jnp
import numpy as np
from jax import lax
from jax.experimental import pallas as pl
from jax.experimental.pallas import tpu as pltpu
from jax.sharding import PartitionSpec as P

NEG = -1e30
MESH = pl.DeviceIdType.MESH


def rotary_tables(rows, blocks, width):
    half = np.arange(width // 2, dtype=np.float64)
    base = 500000.0 ** (-2.0 * half / width)
    wave = 2.0 * np.pi / base
    smooth = (8192.0 / wave - 1.0) / 3.0
    blended = (1.0 - smooth) * base / 8.0 + smooth * base
    freq = np.where(wave < 2048.0, base, np.where(wave > 8192.0, base / 8.0, blended))
    freq = np.concatenate([freq, freq])
    inner = np.arange(rows)[:, None] * freq
    outer = (np.arange(blocks) * rows)[:, None] * freq
    return np.concatenate(
        [np.cos(inner), np.sin(inner), np.cos(outer), np.sin(outer)], axis=0
    ).astype(np.float32)


def each(count, body):
    if count <= 8:
        for index in range(count):
            body(index)
    else:
        lax.fori_loop(0, count, lambda index, _: (body(index), 0)[1], 0)


def kernel(
    plan,
    q_hbm,
    lat_hbm,
    key_up_hbm,
    value_up_hbm,
    docs_hbm,
    table_hbm,
    out_hbm,
    q_buf,
    lat_buf,
    up_buf,
    docs_buf,
    table_buf,
    stage,
    window,
    up_all,
    keys,
    values,
    out_buf,
    row_max,
    total,
    in_sem,
    out_sem,
    send_sem,
    recv_sem,
):
    rows, blocks, back, span, kv, group, width, rank, npb, nka = plan
    slots = back + 1
    pb, ka = lax.axis_index("pb"), lax.axis_index("ka")
    mine_q = pb * nka + ka
    mine_l = ka * npb + pb
    barrier = pltpu.get_barrier_semaphore()

    def greet(slot):
        source = mine_q - back + slot

        @pl.when((source >= 0) & (source != mine_l))
        def _():
            pl.semaphore_signal(
                barrier,
                inc=1,
                device_id={"pb": lax.rem(source, npb), "ka": lax.div(source, npb)},
                device_id_type=MESH,
            )

    each(slots, greet)

    loads = [
        pltpu.make_async_copy(lat_hbm, lat_buf, in_sem.at[0]),
        pltpu.make_async_copy(key_up_hbm, up_buf.at[0], in_sem.at[1]),
        pltpu.make_async_copy(value_up_hbm, up_buf.at[1], in_sem.at[2]),
        pltpu.make_async_copy(docs_hbm, docs_buf, in_sem.at[3]),
        pltpu.make_async_copy(table_hbm, table_buf, in_sem.at[4]),
        pltpu.make_async_copy(q_hbm, q_buf, in_sem.at[5]),
    ]
    for load in loads:
        load.start()

    def clear(slot):
        @pl.when(mine_q - back + slot < 0)
        def _():
            window[slot] = jnp.zeros(window.shape[1:], window.dtype)

    each(slots, clear)

    loads[0].wait()
    place = lax.broadcasted_iota(jnp.int32, (kv * rows, kv * rows), 0)
    col = lax.broadcasted_iota(jnp.int32, (kv * rows, kv * rows), 1)
    pick = jnp.zeros((kv * rows, kv * rows), jnp.float32)
    for g in range(kv):
        here = (place >= g * rows) & (place < (g + 1) * rows)
        pick = jnp.where(here & (col == (place - g * rows) * kv + g), 1.0, pick)
    stage[...] = jnp.dot(
        pick.astype(jnp.bfloat16), lat_buf[...], preferred_element_type=jnp.float32
    ).astype(jnp.bfloat16)

    last = jnp.minimum(blocks - 1, mine_l + back)
    own = ((mine_q >= mine_l) & (mine_q <= last)).astype(jnp.int32)
    partners = last - mine_l + 1 - own

    @pl.when(partners > 0)
    def _():
        pl.semaphore_wait(barrier, partners)

    def copy_to(step):
        target = mine_l + step
        return pltpu.make_async_remote_copy(
            src_ref=stage,
            dst_ref=window.at[back - step],
            send_sem=send_sem.at[step],
            recv_sem=recv_sem.at[back - step],
            device_id={"pb": lax.div(target, nka), "ka": lax.rem(target, nka)},
            device_id_type=MESH,
        )

    def send(step):
        target = mine_l + step

        @pl.when((target < blocks) & (target != mine_q))
        def _():
            copy_to(step).start()

        @pl.when(target == mine_q)
        def _():
            window[back - step] = stage[...]

    each(slots, send)

    loads[1].wait()
    loads[2].wait()
    up_all[...] = jnp.zeros(up_all.shape, up_all.dtype)
    for g in range(kv):
        up_all[g, :rank, :width] = up_buf[0, g]
        up_all[g, rank:, width:] = up_buf[1, g]
    loads[3].wait()
    docs = docs_buf[...]
    query_at = mine_q * rows + lax.broadcasted_iota(jnp.int32, (rows, 1), 0)
    query_at = query_at.astype(jnp.float32)
    begin = jnp.zeros((rows, 1), jnp.float32)
    for doc in range(3):
        cut = jnp.sum(jnp.where(docs <= doc, 1.0, 0.0), axis=0, keepdims=True)
        cut = jnp.sum(cut, axis=1, keepdims=True)
        begin = jnp.maximum(begin, jnp.where(cut <= query_at, cut, 0.0))

    loads[4].wait()
    cos_row, sin_row = table_buf[:rows], table_buf[rows : 2 * rows]
    lane = lax.broadcasted_iota(jnp.int32, (1, width), 1)
    sign = jnp.where(lane < width // 2, -1.0, 1.0)

    def rebuild(slot):
        source = mine_q - back + slot

        @pl.when((source >= 0) & (source != mine_l))
        def _():
            pltpu.make_async_copy(stage, window.at[slot], recv_sem.at[slot]).wait()

        first = jnp.maximum(source, 0)
        cos_block = table_buf[pl.ds(2 * rows + first, 1)]
        sin_block = table_buf[pl.ds(2 * rows + blocks + first, 1)]
        cosine = cos_row * cos_block - sin_row * sin_block
        sine = (sin_row * cos_block + cos_row * sin_block) * sign
        at = slot * rows if isinstance(slot, int) else pl.multiple_of(slot * rows, rows)
        for g in range(kv):
            both = jnp.dot(
                window[slot, g * rows : (g + 1) * rows],
                up_all[g],
                preferred_element_type=jnp.float32,
            )
            key = both[:, :width]
            key = key * cosine + pltpu.roll(key, width // 2, 1) * sine
            keys[g, pl.ds(at, rows)] = key.astype(jnp.bfloat16)
            values[g, pl.ds(at, rows), :width] = both[:, width:].astype(jnp.bfloat16)
            values[g, pl.ds(at, rows), width:] = jnp.ones((rows, width), jnp.bfloat16)

    each(slots, rebuild)

    factor = math.log2(math.e) * width ** (-0.5)
    reach = span * rows
    loads[5].wait()

    def attend(chunk):
        at = chunk * reach if isinstance(chunk, int) else pl.multiple_of(chunk * reach, reach)
        key_at = (mine_q - back + chunk * span) * rows
        key_at = key_at + lax.broadcasted_iota(jnp.int32, (1, reach), 1)
        key_at = key_at.astype(jnp.float32)
        bias = jnp.where((key_at >= begin) & (key_at <= query_at), 0.0, NEG)
        for g in range(kv):
            for h in range(g * group, (g + 1) * group):
                scores = lax.dot_general(
                    q_buf[:, h * width : (h + 1) * width],
                    keys[g, pl.ds(at, reach)],
                    (((1,), (1,)), ((), ())),
                    preferred_element_type=jnp.float32,
                )
                scores = scores + bias
                top = jnp.max(scores, axis=1, keepdims=True)
                if span < slots:
                    before = row_max[h]
                    top = jnp.maximum(top, before)
                    row_max[h] = top
                    scale = jnp.exp2((before - top) * factor)
                weights = jnp.exp2((scores - top) * factor).astype(jnp.bfloat16)
                part = jnp.dot(
                    weights, values[g, pl.ds(at, reach)], preferred_element_type=jnp.float32
                )
                if span < slots:
                    total[h] = total[h] * scale + part
                else:
                    out_buf[:, h * width : (h + 1) * width] = (
                        part[:, :width] / part[:, width:]
                    ).astype(jnp.bfloat16)

    if span < slots:
        row_max[...] = jnp.full(row_max.shape, NEG, jnp.float32)
        total[...] = jnp.zeros(total.shape, jnp.float32)
        lax.fori_loop(0, slots // span, lambda c, _: (attend(c), 0)[1], 0)
        for h in range(kv * group):
            out_buf[:, h * width : (h + 1) * width] = (
                total[h, :, :width] / total[h, :, width:]
            ).astype(jnp.bfloat16)
    else:
        attend(0)
    done = pltpu.make_async_copy(out_buf, out_hbm, out_sem)
    done.start()

    def drain(step):
        target = mine_l + step

        @pl.when((target < blocks) & (target != mine_q))
        def _():
            copy_to(step).wait_send()

    each(slots, drain)
    done.wait()


def shards(queries, latents, key_up, value_up, documents):
    rows = queries.shape[0]
    kv, rank, width = key_up.shape
    heads = queries.shape[1] // width
    npb, nka = lax.axis_size("pb"), lax.axis_size("ka")
    blocks = npb * nka
    tokens = documents.shape[0]
    back = -(-(tokens // 2 - 1) // rows)
    slots = back + 1
    span = max(d for d in range(1, 9) if slots % d == 0)
    many = span < slots
    table = jnp.asarray(rotary_tables(rows, blocks, width))
    plan = (rows, blocks, back, span, kv, heads // kv, width, rank, npb, nka)
    bf16, f32 = jnp.bfloat16, jnp.float32
    return pl.pallas_call(
        functools.partial(kernel, plan),
        out_shape=jax.ShapeDtypeStruct(queries.shape, bf16),
        in_specs=[pl.BlockSpec(memory_space=pltpu.HBM)] * 6,
        out_specs=pl.BlockSpec(memory_space=pltpu.HBM),
        scratch_shapes=[
            pltpu.VMEM(queries.shape, bf16),
            pltpu.VMEM((rows * kv, 2 * rank), bf16),
            pltpu.VMEM((2, kv, rank, width), bf16),
            pltpu.VMEM((tokens // 128, 128), jnp.int32),
            pltpu.VMEM(table.shape, f32),
            pltpu.VMEM((rows * kv, 2 * rank), bf16),
            pltpu.VMEM((slots, rows * kv, 2 * rank), bf16),
            pltpu.VMEM((kv, 2 * rank, 2 * width), bf16),
            pltpu.VMEM((kv, slots * rows, width), bf16),
            pltpu.VMEM((kv, slots * rows, 2 * width), bf16),
            pltpu.VMEM(queries.shape, bf16),
            pltpu.VMEM((heads if many else 1, rows, 1), f32),
            pltpu.VMEM((heads if many else 1, rows, 2 * width), f32),
            pltpu.SemaphoreType.DMA((6,)),
            pltpu.SemaphoreType.DMA,
            pltpu.SemaphoreType.DMA((slots,)),
            pltpu.SemaphoreType.DMA((slots,)),
        ],
        compiler_params=pltpu.CompilerParams(
            collective_id=0, has_side_effects=True, vmem_limit_bytes=63 * 2**20
        ),
    )(
        queries,
        latents.reshape(rows * kv, 2 * rank),
        key_up,
        value_up,
        documents.reshape(tokens // 128, 128),
        table,
    )


def solution(mesh):
    placed = (
        P(("pb", "ka"), "ha"),
        P(("ka", "pb"), "ha", None),
        P("ha", None, None),
        P("ha", None, None),
        P(),
    )
    return jax.shard_map(
        shards, mesh=mesh, in_specs=placed, out_specs=P(("pb", "ka"), "ha"), check_vma=False
    )
```

profile of v0, /device:TPU:6, one launch (start us, length us, event | category | flops | bytes accessed | tf_op | source)
XLA Modules:
  0.0 12.4 jit_solution(7015317126732616699)
XLA Ops:
  0.0 10.8 %shard_map.64 = bf16[96,1024]{1,0:T(8,128)(2,1)} custom-call(bf16[96,1024]{1,0:T(8,128)(2,1)} %q_hbm.1, bf16[192,128]{1,0:T(8,128)(2,1)} %bitcast.2, bf16[2,64,128]{2,1,0:T(8,128)(2,1)} %key_up_hbm.1, bf16[2,64,128]{2,1,0:T(8,128)(2,1)} %value_up_hbm.1, s32[6,128]{1,0:T(8,128)} %bitcast.3, f32[208,128]{1,0:T(8,128)} %constant.2.clone.table_hbm), custom_call_target="tpu_custom_call" | custom-call | tf_op jit(solution)/shard_map/pallas_call | solution.py:270
  10.8 1.6 %copy.8 = bf16[96,1024]{1,0:T(8,128)(2,1)} copy(bf16[96,1024]{1,0:T(8,128)(2,1)} %shard_map.64) | data formatting | bytes 393216
where the time goes:
time: 12.5 us; the launch traced here: 12.4 us
  Pallas kernels  10.8 us (86%)
  local copies, waits for them, and re-layouts  1.62 us (13%)
    pallas_call x1, Pallas kernels, shards(): pl.pallas_call(functools.partial(kernel, plan), out_shape=jax.ShapeDtypeS...  10.8 us
    unnamed x1, local copies, waits for them, and re-layouts  1.62 us

commit v1 on v0

--- a/solution.py
+++ b/solution.py
@@ -44,7 +44,7 @@
     value_up_hbm,
     docs_hbm,
     table_hbm,
-    out_hbm,
+    out_ref,
     q_buf,
     lat_buf,
     up_buf,
@@ -55,11 +55,9 @@
     up_all,
     keys,
     values,
-    out_buf,
     row_max,
     total,
     in_sem,
-    out_sem,
     send_sem,
     recv_sem,
 ):
@@ -203,44 +201,46 @@
         key_at = key_at + lax.broadcasted_iota(jnp.int32, (1, reach), 1)
         key_at = key_at.astype(jnp.float32)
         bias = jnp.where((key_at >= begin) & (key_at <= query_at), 0.0, NEG)
+        bias = jnp.concatenate([bias] * group, axis=0)
         for g in range(kv):
-            for h in range(g * group, (g + 1) * group):
-                scores = lax.dot_general(
-                    q_buf[:, h * width : (h + 1) * width],
-                    keys[g, pl.ds(at, reach)],
-                    (((1,), (1,)), ((), ())),
-                    preferred_element_type=jnp.float32,
-                )
-                scores = scores + bias
-                top = jnp.max(scores, axis=1, keepdims=True)
-                if span < slots:
-                    before = row_max[h]
-                    top = jnp.maximum(top, before)
-                    row_max[h] = top
-                    scale = jnp.exp2((before - top) * factor)
-                weights = jnp.exp2((scores - top) * factor).astype(jnp.bfloat16)
-                part = jnp.dot(
-                    weights, values[g, pl.ds(at, reach)], preferred_element_type=jnp.float32
-                )
-                if span < slots:
-                    total[h] = total[h] * scale + part
-                else:
-                    out_buf[:, h * width : (h + 1) * width] = (
-                        part[:, :width] / part[:, width:]
-                    ).astype(jnp.bfloat16)
+            heads = range(g * group, (g + 1) * group)
+            stacked = jnp.concatenate([q_buf[:, h * width : (h + 1) * width] for h in heads])
+            scores = lax.dot_general(
+                stacked,
+                keys[g, pl.ds(at, reach)],
+                (((1,), (1,)), ((), ())),
+                preferred_element_type=jnp.float32,
+            )
+            scores = scores + bias
+            top = jnp.max(scores, axis=1, keepdims=True)
+            if span < slots:
+                before = row_max[g]
+                top = jnp.maximum(top, before)
+                row_max[g] = top
+                scale = jnp.exp2((before - top) * factor)
+            weights = jnp.exp2((scores - top) * factor).astype(jnp.bfloat16)
+            part = jnp.dot(
+                weights, values[g, pl.ds(at, reach)], preferred_element_type=jnp.float32
+            )
+            if span < slots:
+                total[g] = total[g] * scale + part
+            else:
+                write(g, part)
+
+    def write(g, part):
+        ratio = (part[:, :width] / part[:, width:]).astype(jnp.bfloat16)
+        for i in range(group):
+            h = g * group + i
+            out_ref[:, h * width : (h + 1) * width] = ratio[i * rows : (i + 1) * rows]
 
     if span < slots:
         row_max[...] = jnp.full(row_max.shape, NEG, jnp.float32)
         total[...] = jnp.zeros(total.shape, jnp.float32)
         lax.fori_loop(0, slots // span, lambda c, _: (attend(c), 0)[1], 0)
-        for h in range(kv * group):
-            out_buf[:, h * width : (h + 1) * width] = (
-                total[h, :, :width] / total[h, :, width:]
-            ).astype(jnp.bfloat16)
+        for g in range(kv):
+            write(g, total[g])
     else:
         attend(0)
-    done = pltpu.make_async_copy(out_buf, out_hbm, out_sem)
-    done.start()
 
     def drain(step):
         target = mine_l + step
@@ -250,7 +250,6 @@
             copy_to(step).wait_send()
 
     each(slots, drain)
-    done.wait()
 
 
 def shards(queries, latents, key_up, value_up, documents):
@@ -269,9 +268,9 @@
     bf16, f32 = jnp.bfloat16, jnp.float32
     return pl.pallas_call(
         functools.partial(kernel, plan),
-        out_shape=jax.ShapeDtypeStruct(queries.shape, bf16),
+        out_shape=pltpu.VMEM(queries.shape, bf16),
         in_specs=[pl.BlockSpec(memory_space=pltpu.HBM)] * 6,
-        out_specs=pl.BlockSpec(memory_space=pltpu.HBM),
+        out_specs=pl.BlockSpec(memory_space=pltpu.VMEM),
         scratch_shapes=[
             pltpu.VMEM(queries.shape, bf16),
             pltpu.VMEM((rows * kv, 2 * rank), bf16),
@@ -283,11 +282,9 @@
             pltpu.VMEM((kv, 2 * rank, 2 * width), bf16),
             pltpu.VMEM((kv, slots * rows, width), bf16),
             pltpu.VMEM((kv, slots * rows, 2 * width), bf16),
-            pltpu.VMEM(queries.shape, bf16),
-            pltpu.VMEM((heads if many else 1, rows, 1), f32),
-            pltpu.VMEM((heads if many else 1, rows, 2 * width), f32),
+            pltpu.VMEM((kv, heads // kv * rows if many else 8, 1), f32),
+            pltpu.VMEM((kv, heads // kv * rows if many else 8, 2 * width), f32),
             pltpu.SemaphoreType.DMA((6,)),
-            pltpu.SemaphoreType.DMA,
             pltpu.SemaphoreType.DMA((slots,)),
             pltpu.SemaphoreType.DMA((slots,)),
         ],

time: 12.5 us -> 9.26 us (0.74)
  Pallas kernels: 10.8 us -> 8.43 us
  local copies, waits for them, and re-layouts: 1.62 us -> 0.68 us
    pallas_call x1, Pallas kernels: 10.8 us -> 8.43 us  [shards(): pl.pallas_call(functools.partial(kernel, plan), out_shape=pltpu.VMEM(quer...]
    unnamed x1, local copies, waits for them, and re-layouts: 1.62 us -> 0.68 us
where the time goes in v1:
time: 9.26 us; the launch traced here: 9.11 us
  Pallas kernels  8.43 us (91%)
  local copies, waits for them, and re-layouts  0.68 us (7%)
    pallas_call x1, Pallas kernels, shards(): pl.pallas_call(functools.partial(kernel, plan), out_shape=pltpu.VMEM(quer...  8.43 us
    unnamed x1, local copies, waits for them, and re-layouts  0.68 us

profile of v1, /device:TPU:6, one launch (start us, length us, event | category | flops | bytes accessed | tf_op | source)
XLA Modules:
  0.0 9.1 jit_solution(18024842536662712327)
XLA Ops:
  0.0 8.4 %shard_map.64 = bf16[96,1024]{1,0:T(8,128)(2,1)S(1)} custom-call(bf16[96,1024]{1,0:T(8,128)(2,1)} %q_hbm.1, bf16[192,128]{1,0:T(8,128)(2,1)} %bitcast.2, bf16[2,64,128]{2,1,0:T(8,128)(2,1)} %key_up_hbm.1, bf16[2,64,128]{2,1,0:T(8,128)(2,1)} %value_up_hbm.1, s32[6,128]{1,0:T(8,128)} %bitcast.3, f32[208,128]{1,0:T(8,128)} %constant.2.clone.table_hbm), custom_call_target="tpu_custom_call" | custom-call | tf_op jit(solution)/shard_map/pallas_call | solution.py:269
  8.4 0.7 %copy.8 = bf16[96,1024]{1,0:T(8,128)(2,1)} copy(bf16[96,1024]{1,0:T(8,128)(2,1)S(1)} %shard_map.64) | data formatting | bytes 393216

commit v2 on v1

--- a/solution.py
+++ b/solution.py
@@ -46,11 +46,12 @@
     table_hbm,
     out_ref,
     q_buf,
-    lat_buf,
     up_buf,
     docs_buf,
     table_buf,
-    stage,
+    pick,
+    cosines,
+    sines,
     window,
     up_all,
     keys,
@@ -60,96 +61,113 @@
     in_sem,
     send_sem,
     recv_sem,
+    pass_sem,
+    mate_sem,
 ):
     rows, blocks, back, span, kv, group, width, rank, npb, nka = plan
     slots = back + 1
+    half = rows * kv // 2
     pb, ka = lax.axis_index("pb"), lax.axis_index("ka")
     mine_q = pb * nka + ka
     mine_l = ka * npb + pb
+    core = lax.rem(ka, 2)
+    pair = lax.div(mine_q, 2)
+    mate = ka + 1 - 2 * core
+    base = 2 * pair - back
     barrier = pltpu.get_barrier_semaphore()
 
+    def greet_at(at_pb, at_ka):
+        pl.semaphore_signal(
+            barrier, inc=1, device_id={"pb": at_pb, "ka": at_ka}, device_id_type=MESH
+        )
+
     def greet(slot):
-        source = mine_q - back + slot
+        source = base + slot
 
         @pl.when((source >= 0) & (source != mine_l))
         def _():
-            pl.semaphore_signal(
-                barrier,
-                inc=1,
-                device_id={"pb": lax.rem(source, npb), "ka": lax.div(source, npb)},
-                device_id_type=MESH,
-            )
-
-    each(slots, greet)
+            greet_at(lax.rem(source, npb), lax.div(source, npb))
+
+    each(slots + 1, greet)
+    mate_l = mate * npb + pb
+    mate_apart = (mate_l < base) | (mate_l > 2 * pair + 1)
+
+    @pl.when(mate_apart)
+    def _():
+        greet_at(pb, mate)
 
     loads = [
-        pltpu.make_async_copy(lat_hbm, lat_buf, in_sem.at[0]),
-        pltpu.make_async_copy(key_up_hbm, up_buf.at[0], in_sem.at[1]),
-        pltpu.make_async_copy(value_up_hbm, up_buf.at[1], in_sem.at[2]),
-        pltpu.make_async_copy(docs_hbm, docs_buf, in_sem.at[3]),
-        pltpu.make_async_copy(table_hbm, table_buf, in_sem.at[4]),
-        pltpu.make_async_copy(q_hbm, q_buf, in_sem.at[5]),
+        pltpu.make_async_copy(docs_hbm, docs_buf, in_sem.at[0]),
+        pltpu.make_async_copy(table_hbm, table_buf, in_sem.at[1]),
+        pltpu.make_async_copy(key_up_hbm, up_buf.at[0], in_sem.at[2]),
+        pltpu.make_async_copy(value_up_hbm, up_buf.at[1], in_sem.at[3]),
+        pltpu.make_async_copy(q_hbm, q_buf, in_sem.at[4]),
     ]
     for load in loads:
         load.start()
 
+    def part_of(ref, which):
+        return ref.at[pl.ds(pl.multiple_of(which * half, half), half)]
+
+    def take_own(slot):
+        return pltpu.make_async_copy(
+            part_of(lat_hbm, core), part_of(window.at[slot], core), recv_sem.at[slot]
+        )
+
+    def keep(slot):
+        @pl.when(base + slot == mine_l)
+        def _():
+            take_own(slot).start()
+
+    each(slots + 1, keep)
+
+    first_pair = lax.div(mine_l, 2)
+    last_pair = jnp.minimum(blocks // 2 - 1, lax.div(mine_l + back, 2))
+    inside = ((pair >= first_pair) & (pair <= last_pair)).astype(jnp.int32)
+    pl.semaphore_wait(barrier, 2 * (last_pair - first_pair + 1) + 1 - 2 * inside)
+
+    def copy_to(step):
+        target, side = first_pair + step // 2, step % 2
+        slot = mine_l - 2 * target + back
+        other = 2 * target + side
+        return pltpu.make_async_remote_copy(
+            src_ref=lat_hbm.at[pl.ds(side * half, half)],
+            dst_ref=window.at[slot, pl.ds(side * half, half)],
+            send_sem=send_sem.at[step],
+            recv_sem=recv_sem.at[slot],
+            device_id={"pb": lax.div(other, nka), "ka": lax.rem(other, nka)},
+            device_id_type=MESH,
+        )
+
+    reached = 2 * (back // 2 + 1 + back % 2)
+
+    def goes(step):
+        target = first_pair + step // 2
+        return (target <= last_pair) & (2 * target + step % 2 != mine_q)
+
+    def send(step):
+        @pl.when(goes(step))
+        def _():
+            copy_to(step).start()
+
+    each(reached, send)
+
     def clear(slot):
-        @pl.when(mine_q - back + slot < 0)
+        @pl.when(base + slot < 0)
         def _():
             window[slot] = jnp.zeros(window.shape[1:], window.dtype)
 
-    each(slots, clear)
-
-    loads[0].wait()
+    each(slots + 1, clear)
+    values[:, :, width:] = jnp.ones((kv, slots * rows, width), jnp.bfloat16)
+    up_all[...] = jnp.zeros(up_all.shape, up_all.dtype)
     place = lax.broadcasted_iota(jnp.int32, (kv * rows, kv * rows), 0)
     col = lax.broadcasted_iota(jnp.int32, (kv * rows, kv * rows), 1)
-    pick = jnp.zeros((kv * rows, kv * rows), jnp.float32)
+    sort = jnp.zeros((kv * rows, kv * rows), jnp.float32)
     for g in range(kv):
         here = (place >= g * rows) & (place < (g + 1) * rows)
-        pick = jnp.where(here & (col == (place - g * rows) * kv + g), 1.0, pick)
-    stage[...] = jnp.dot(
-        pick.astype(jnp.bfloat16), lat_buf[...], preferred_element_type=jnp.float32
-    ).astype(jnp.bfloat16)
-
-    last = jnp.minimum(blocks - 1, mine_l + back)
-    own = ((mine_q >= mine_l) & (mine_q <= last)).astype(jnp.int32)
-    partners = last - mine_l + 1 - own
-
-    @pl.when(partners > 0)
-    def _():
-        pl.semaphore_wait(barrier, partners)
-
-    def copy_to(step):
-        target = mine_l + step
-        return pltpu.make_async_remote_copy(
-            src_ref=stage,
-            dst_ref=window.at[back - step],
-            send_sem=send_sem.at[step],
-            recv_sem=recv_sem.at[back - step],
-            device_id={"pb": lax.div(target, nka), "ka": lax.rem(target, nka)},
-            device_id_type=MESH,
-        )
-
-    def send(step):
-        target = mine_l + step
-
-        @pl.when((target < blocks) & (target != mine_q))
-        def _():
-            copy_to(step).start()
-
-        @pl.when(target == mine_q)
-        def _():
-            window[back - step] = stage[...]
-
-    each(slots, send)
-
-    loads[1].wait()
-    loads[2].wait()
-    up_all[...] = jnp.zeros(up_all.shape, up_all.dtype)
-    for g in range(kv):
-        up_all[g, :rank, :width] = up_buf[0, g]
-        up_all[g, rank:, width:] = up_buf[1, g]
-    loads[3].wait()
+        sort = jnp.where(here & (col == (place - g * rows) * kv + g), 1.0, sort)
+    pick[...] = sort.astype(jnp.bfloat16)
+    loads[0].wait()
     docs = docs_buf[...]
     query_at = mine_q * rows + lax.broadcasted_iota(jnp.int32, (rows, 1), 0)
     query_at = query_at.astype(jnp.float32)
@@ -159,41 +177,82 @@
         cut = jnp.sum(cut, axis=1, keepdims=True)
         begin = jnp.maximum(begin, jnp.where(cut <= query_at, cut, 0.0))
 
-    loads[4].wait()
+    loads[1].wait()
     cos_row, sin_row = table_buf[:rows], table_buf[rows : 2 * rows]
     lane = lax.broadcasted_iota(jnp.int32, (1, width), 1)
     sign = jnp.where(lane < width // 2, -1.0, 1.0)
 
-    def rebuild(slot):
-        source = mine_q - back + slot
-
-        @pl.when((source >= 0) & (source != mine_l))
-        def _():
-            pltpu.make_async_copy(stage, window.at[slot], recv_sem.at[slot]).wait()
-
-        first = jnp.maximum(source, 0)
+    def row_of(slot):
+        return slot * rows if isinstance(slot, int) else pl.multiple_of(slot * rows, rows)
+
+    def angles(slot):
+        first = jnp.maximum(mine_q - back + slot, 0)
         cos_block = table_buf[pl.ds(2 * rows + first, 1)]
         sin_block = table_buf[pl.ds(2 * rows + blocks + first, 1)]
-        cosine = cos_row * cos_block - sin_row * sin_block
-        sine = (sin_row * cos_block + cos_row * sin_block) * sign
-        at = slot * rows if isinstance(slot, int) else pl.multiple_of(slot * rows, rows)
+        cosines[pl.ds(row_of(slot), rows)] = cos_row * cos_block - sin_row * sin_block
+        sines[pl.ds(row_of(slot), rows)] = (sin_row * cos_block + cos_row * sin_block) * sign
+
+    each(slots, angles)
+    loads[2].wait()
+    loads[3].wait()
+    for g in range(kv):
+        up_all[g, :rank, :width] = up_buf[0, g]
+        up_all[g, rank:, width:] = up_buf[1, g]
+    loads[4].wait()
+
+    def hand_on(slot):
+        return pltpu.make_async_remote_copy(
+            src_ref=part_of(window.at[slot], core),
+            dst_ref=part_of(window.at[slot], core),
+            send_sem=pass_sem.at[slot],
+            recv_sem=mate_sem.at[slot],
+            device_id={"pb": pb, "ka": mate},
+            device_id_type=MESH,
+        )
+
+    def mate_needs(slot):
+        return (base + slot >= 0) & (slot >= 1 - core) & (slot <= 1 - core + back)
+
+    def relay(slot):
+        @pl.when(base + slot >= 0)
+        def _():
+            take_own(slot).wait()
+
+        @pl.when(mate_needs(slot))
+        def _():
+            hand_on(slot).start()
+
+    each(slots + 1, relay)
+
+    def rebuild(slot):
+        at = row_of(slot)
+        where = core + slot
+
+        @pl.when(base + where >= 0)
+        def _():
+            pltpu.make_async_copy(
+                part_of(lat_hbm, 1 - core), part_of(window.at[where], 1 - core), mate_sem.at[where]
+            ).wait()
+
+        sorted_rows = jnp.dot(
+            pick[...], window[where], preferred_element_type=jnp.float32
+        ).astype(jnp.bfloat16)
         for g in range(kv):
             both = jnp.dot(
-                window[slot, g * rows : (g + 1) * rows],
+                sorted_rows[g * rows : (g + 1) * rows],
                 up_all[g],
                 preferred_element_type=jnp.float32,
             )
             key = both[:, :width]
-            key = key * cosine + pltpu.roll(key, width // 2, 1) * sine
+            key = key * cosines[pl.ds(at, rows)]
+            key = key + pltpu.roll(both[:, :width], width // 2, 1) * sines[pl.ds(at, rows)]
             keys[g, pl.ds(at, rows)] = key.astype(jnp.bfloat16)
             values[g, pl.ds(at, rows), :width] = both[:, width:].astype(jnp.bfloat16)
-            values[g, pl.ds(at, rows), width:] = jnp.ones((rows, width), jnp.bfloat16)
 
     each(slots, rebuild)
 
     factor = math.log2(math.e) * width ** (-0.5)
     reach = span * rows
-    loads[5].wait()
 
     def attend(chunk):
         at = chunk * reach if isinstance(chunk, int) else pl.multiple_of(chunk * reach, reach)
@@ -243,13 +302,18 @@
         attend(0)
 
     def drain(step):
-        target = mine_l + step
-
-        @pl.when((target < blocks) & (target != mine_q))
+        @pl.when(goes(step))
         def _():
             copy_to(step).wait_send()
 
-    each(slots, drain)
+    each(reached, drain)
+
+    def drain_mate(slot):
+        @pl.when(mate_needs(slot))
+        def _():
+            hand_on(slot).wait_send()
+
+    each(slots + 1, drain_mate)
 
 
 def shards(queries, latents, key_up, value_up, documents):
@@ -273,20 +337,23 @@
         out_specs=pl.BlockSpec(memory_space=pltpu.VMEM),
         scratch_shapes=[
             pltpu.VMEM(queries.shape, bf16),
-            pltpu.VMEM((rows * kv, 2 * rank), bf16),
             pltpu.VMEM((2, kv, rank, width), bf16),
             pltpu.VMEM((tokens // 128, 128), jnp.int32),
             pltpu.VMEM(table.shape, f32),
-            pltpu.VMEM((rows * kv, 2 * rank), bf16),
-            pltpu.VMEM((slots, rows * kv, 2 * rank), bf16),
+            pltpu.VMEM((rows * kv, rows * kv), bf16),
+            pltpu.VMEM((slots * rows, width), f32),
+            pltpu.VMEM((slots * rows, width), f32),
+            pltpu.VMEM((slots + 1, rows * kv, 2 * rank), bf16),
             pltpu.VMEM((kv, 2 * rank, 2 * width), bf16),
             pltpu.VMEM((kv, slots * rows, width), bf16),
             pltpu.VMEM((kv, slots * rows, 2 * width), bf16),
             pltpu.VMEM((kv, heads // kv * rows if many else 8, 1), f32),
             pltpu.VMEM((kv, heads // kv * rows if many else 8, 2 * width), f32),
-            pltpu.SemaphoreType.DMA((6,)),
-            pltpu.SemaphoreType.DMA((slots,)),
-            pltpu.SemaphoreType.DMA((slots,)),
+            pltpu.SemaphoreType.DMA((5,)),
+            pltpu.SemaphoreType.DMA((slots + 2,)),
+            pltpu.SemaphoreType.DMA((slots + 1,)),
+            pltpu.SemaphoreType.DMA((slots + 1,)),
+            pltpu.SemaphoreType.DMA((slots + 1,)),
         ],
         compiler_params=pltpu.CompilerParams(
             collective_id=0, has_side_effects=True, vmem_limit_bytes=63 * 2**20

time: 9.26 us -> 10.2 us (1.10)
  the two profiles are of different devices: /device:TPU:6 before, /device:TPU:7 now
where the time goes in v2:
time: 10.2 us; the launch traced here: 10.1 us
  Pallas kernels  9.41 us (92%)
  local copies, waits for them, and re-layouts  0.68 us (7%)
    pallas_call x1, Pallas kernels, shards(): pl.pallas_call(functools.partial(kernel, plan), out_shape=pltpu.VMEM(quer...  9.41 us
    unnamed x1, local copies, waits for them, and re-layouts  0.68 us

profile of v2, /device:TPU:7, one launch (start us, length us, event | category | flops | bytes accessed | tf_op | source)
XLA Modules:
  0.0 10.1 jit_solution(13566296393930652360)
XLA Ops:
  0.0 9.4 %shard_map.64 = bf16[96,1024]{1,0:T(8,128)(2,1)S(1)} custom-call(bf16[96,1024]{1,0:T(8,128)(2,1)} %q_hbm.1, bf16[192,128]{1,0:T(8,128)(2,1)} %bitcast.2, bf16[2,64,128]{2,1,0:T(8,128)(2,1)} %key_up_hbm.1, bf16[2,64,128]{2,1,0:T(8,128)(2,1)} %value_up_hbm.1, s32[6,128]{1,0:T(8,128)} %bitcast.3, f32[208,128]{1,0:T(8,128)} %constant.2.clone.table_hbm), custom_call_target="tpu_custom_call" | custom-call | tf_op jit(solution)/shard_map/pallas_call | solution.py:333
  9.4 0.7 %copy.8 = bf16[96,1024]{1,0:T(8,128)(2,1)} copy(bf16[96,1024]{1,0:T(8,128)(2,1)S(1)} %shard_map.64) | data formatting | bytes 393216

commit v3 on v1

--- a/solution.py
+++ b/solution.py
@@ -26,6 +26,12 @@
     return np.concatenate(
         [np.cos(inner), np.sin(inner), np.cos(outer), np.sin(outer)], axis=0
     ).astype(np.float32)
+
+
+def split(number, size):
+    if size & (size - 1):
+        return lax.div(number, size), lax.rem(number, size)
+    return lax.shift_right_logical(number, size.bit_length() - 1), number & (size - 1)
 
 
 def each(count, body):
@@ -52,6 +58,8 @@
     table_buf,
     stage,
     window,
+    cosines,
+    sines,
     up_all,
     keys,
     values,
@@ -73,11 +81,9 @@
 
         @pl.when((source >= 0) & (source != mine_l))
         def _():
+            at_ka, at_pb = split(source, npb)
             pl.semaphore_signal(
-                barrier,
-                inc=1,
-                device_id={"pb": lax.rem(source, npb), "ka": lax.div(source, npb)},
-                device_id_type=MESH,
+                barrier, inc=1, device_id={"pb": at_pb, "ka": at_ka}, device_id_type=MESH
             )
 
     each(slots, greet)
@@ -120,13 +126,13 @@
         pl.semaphore_wait(barrier, partners)
 
     def copy_to(step):
-        target = mine_l + step
+        at_pb, at_ka = split(mine_l + step, nka)
         return pltpu.make_async_remote_copy(
             src_ref=stage,
             dst_ref=window.at[back - step],
             send_sem=send_sem.at[step],
             recv_sem=recv_sem.at[back - step],
-            device_id={"pb": lax.div(target, nka), "ka": lax.rem(target, nka)},
+            device_id={"pb": at_pb, "ka": at_ka},
             device_id_type=MESH,
         )
 
@@ -164,68 +170,65 @@
     lane = lax.broadcasted_iota(jnp.int32, (1, width), 1)
     sign = jnp.where(lane < width // 2, -1.0, 1.0)
 
-    def rebuild(slot):
-        source = mine_q - back + slot
-
-        @pl.when((source >= 0) & (source != mine_l))
-        def _():
-            pltpu.make_async_copy(stage, window.at[slot], recv_sem.at[slot]).wait()
-
-        first = jnp.maximum(source, 0)
+    def row_of(slot):
+        return slot * rows if isinstance(slot, int) else pl.multiple_of(slot * rows, rows)
+
+    def angles(slot):
+        first = jnp.maximum(mine_q - back + slot, 0)
         cos_block = table_buf[pl.ds(2 * rows + first, 1)]
         sin_block = table_buf[pl.ds(2 * rows + blocks + first, 1)]
-        cosine = cos_row * cos_block - sin_row * sin_block
-        sine = (sin_row * cos_block + cos_row * sin_block) * sign
-        at = slot * rows if isinstance(slot, int) else pl.multiple_of(slot * rows, rows)
+        cosines[pl.ds(row_of(slot), rows)] = cos_row * cos_block - sin_row * sin_block
+        sines[pl.ds(row_of(slot), rows)] = (sin_row * cos_block + cos_row * sin_block) * sign
+
+    each(slots, angles)
+    values[:, :, width:] = jnp.ones((kv, slots * rows, width), jnp.bfloat16)
+
+    def bias_of(first, count):
+        key_at = (mine_q - back + first) * rows
+        key_at = key_at + lax.broadcasted_iota(jnp.int32, (1, count * rows), 1)
+        key_at = key_at.astype(jnp.float32)
+        return jnp.where((key_at >= begin) & (key_at <= query_at), 0.0, NEG)
+
+    def arrive(slot):
+        source = mine_q - back + slot
+
+        @pl.when((source >= 0) & (source != mine_l))
+        def _():
+            pltpu.make_async_copy(stage, window.at[slot], recv_sem.at[slot]).wait()
+
+    def rebuild(first, count):
+        at, reach = row_of(first), count * rows
         for g in range(kv):
+            latents = [window[first + i, g * rows : (g + 1) * rows] for i in range(count)]
             both = jnp.dot(
-                window[slot, g * rows : (g + 1) * rows],
-                up_all[g],
-                preferred_element_type=jnp.float32,
+                jnp.concatenate(latents), up_all[g], preferred_element_type=jnp.float32
             )
-            key = both[:, :width]
-            key = key * cosine + pltpu.roll(key, width // 2, 1) * sine
-            keys[g, pl.ds(at, rows)] = key.astype(jnp.bfloat16)
-            values[g, pl.ds(at, rows), :width] = both[:, width:].astype(jnp.bfloat16)
-            values[g, pl.ds(at, rows), width:] = jnp.ones((rows, width), jnp.bfloat16)
-
-    each(slots, rebuild)
+            key = both[:, :width] * cosines[pl.ds(at, reach)]
+            key = key + pltpu.roll(both[:, :width], width // 2, 1) * sines[pl.ds(at, reach)]
+            keys[g, pl.ds(at, reach)] = key.astype(jnp.bfloat16)
+            values[g, pl.ds(at, reach), :width] = both[:, width:].astype(jnp.bfloat16)
 
     factor = math.log2(math.e) * width ** (-0.5)
-    reach = span * rows
-    loads[5].wait()
-
-    def attend(chunk):
-        at = chunk * reach if isinstance(chunk, int) else pl.multiple_of(chunk * reach, reach)
-        key_at = (mine_q - back + chunk * span) * rows
-        key_at = key_at + lax.broadcasted_iota(jnp.int32, (1, reach), 1)
-        key_at = key_at.astype(jnp.float32)
-        bias = jnp.where((key_at >= begin) & (key_at <= query_at), 0.0, NEG)
-        bias = jnp.concatenate([bias] * group, axis=0)
-        for g in range(kv):
-            heads = range(g * group, (g + 1) * group)
-            stacked = jnp.concatenate([q_buf[:, h * width : (h + 1) * width] for h in heads])
-            scores = lax.dot_general(
-                stacked,
-                keys[g, pl.ds(at, reach)],
-                (((1,), (1,)), ((), ())),
-                preferred_element_type=jnp.float32,
-            )
-            scores = scores + bias
-            top = jnp.max(scores, axis=1, keepdims=True)
-            if span < slots:
-                before = row_max[g]
-                top = jnp.maximum(top, before)
-                row_max[g] = top
-                scale = jnp.exp2((before - top) * factor)
-            weights = jnp.exp2((scores - top) * factor).astype(jnp.bfloat16)
-            part = jnp.dot(
-                weights, values[g, pl.ds(at, reach)], preferred_element_type=jnp.float32
-            )
-            if span < slots:
-                total[g] = total[g] * scale + part
-            else:
-                write(g, part)
+
+    def attend(g, first, count, bias, before, sums):
+        at, reach = row_of(first), count * rows
+        heads = range(g * group, (g + 1) * group)
+        stacked = jnp.concatenate([q_buf[:, h * width : (h + 1) * width] for h in heads])
+        scores = lax.dot_general(
+            stacked,
+            keys[g, pl.ds(at, reach)],
+            (((1,), (1,)), ((), ())),
+            preferred_element_type=jnp.float32,
+        )
+        scores = scores + jnp.concatenate([bias] * group)
+        top = jnp.max(scores, axis=1, keepdims=True)
+        if before is not None:
+            top = jnp.maximum(top, before)
+        weights = jnp.exp2((scores - top) * factor).astype(jnp.bfloat16)
+        part = jnp.dot(weights, values[g, pl.ds(at, reach)], preferred_element_type=jnp.float32)
+        if before is not None:
+            part = part + sums * jnp.exp2((before - top) * factor)
+        return top, part
 
     def write(g, part):
         ratio = (part[:, :width] / part[:, width:]).astype(jnp.bfloat16)
@@ -233,23 +236,43 @@
             h = g * group + i
             out_ref[:, h * width : (h + 1) * width] = ratio[i * rows : (i + 1) * rows]
 
-    if span < slots:
+    def drain(step):
+        target = mine_l + step
+
+        @pl.when((target < blocks) & (target != mine_q))
+        def _():
+            copy_to(step).wait_send()
+
+    if slots <= 8:
+        mask = bias_of(0, slots)
+        loads[5].wait()
+        for slot in reversed(range(slots)):
+            arrive(slot)
+            if slot == 1:
+                each(slots, drain)
+        rebuild(0, slots)
+        for g in range(kv):
+            write(g, attend(g, 0, slots, mask, None, None)[1])
+    else:
         row_max[...] = jnp.full(row_max.shape, NEG, jnp.float32)
         total[...] = jnp.zeros(total.shape, jnp.float32)
-        lax.fori_loop(0, slots // span, lambda c, _: (attend(c), 0)[1], 0)
+        loads[5].wait()
+
+        def run(chunk, _):
+            for i in range(span):
+                arrive(chunk * span + i)
+            rebuild(chunk * span, span)
+            mask = bias_of(chunk * span, span)
+            for g in range(kv):
+                row_max[g], total[g] = attend(
+                    g, chunk * span, span, mask, row_max[g], total[g]
+                )
+            return 0
+
+        lax.fori_loop(0, slots // span, run, 0)
         for g in range(kv):
             write(g, total[g])
-    else:
-        attend(0)
-
-    def drain(step):
-        target = mine_l + step
-
-        @pl.when((target < blocks) & (target != mine_q))
-        def _():
-            copy_to(step).wait_send()
-
-    each(slots, drain)
+        each(slots, drain)
 
 
 def shards(queries, latents, key_up, value_up, documents):
@@ -262,7 +285,7 @@
     back = -(-(tokens // 2 - 1) // rows)
     slots = back + 1
     span = max(d for d in range(1, 9) if slots % d == 0)
-    many = span < slots
+    many = slots > 8
     table = jnp.asarray(rotary_tables(rows, blocks, width))
     plan = (rows, blocks, back, span, kv, heads // kv, width, rank, npb, nka)
     bf16, f32 = jnp.bfloat16, jnp.float32
@@ -279,6 +302,8 @@
             pltpu.VMEM(table.shape, f32),
             pltpu.VMEM((rows * kv, 2 * rank), bf16),
             pltpu.VMEM((slots, rows * kv, 2 * rank), bf16),
+            pltpu.VMEM((slots * rows, width), f32),
+            pltpu.VMEM((slots * rows, width), f32),
             pltpu.VMEM((kv, 2 * rank, 2 * width), bf16),
             pltpu.VMEM((kv, slots * rows, width), bf16),
             pltpu.VMEM((kv, slots * rows, 2 * width), bf16),

time: 9.26 us -> 8.66 us (0.935)
  the two profiles are of different devices: /device:TPU:6 before, /device:TPU:11 now
where the time goes in v3:
time: 8.66 us; the launch traced here: 8.52 us
  Pallas kernels  7.83 us (90%)
  local copies, waits for them, and re-layouts  0.68 us (8%)
    pallas_call x1, Pallas kernels, shards(): pl.pallas_call(functools.partial(kernel, plan), out_shape=pltpu.VMEM(quer...  7.83 us
    unnamed x1, local copies, waits for them, and re-layouts  0.68 us

profile of v3, /device:TPU:11, one launch (start us, length us, event | category | flops | bytes accessed | tf_op | source)
XLA Modules:
  0.0 8.5 jit_solution(13865554749543985849)
XLA Ops:
  0.0 7.8 %shard_map.64 = bf16[96,1024]{1,0:T(8,128)(2,1)S(1)} custom-call(bf16[96,1024]{1,0:T(8,128)(2,1)} %q_hbm.1, bf16[192,128]{1,0:T(8,128)(2,1)} %bitcast.2, bf16[2,64,128]{2,1,0:T(8,128)(2,1)} %key_up_hbm.1, bf16[2,64,128]{2,1,0:T(8,128)(2,1)} %value_up_hbm.1, s32[6,128]{1,0:T(8,128)} %bitcast.3, f32[208,128]{1,0:T(8,128)} %constant.2.clone.table_hbm), custom_call_target="tpu_custom_call" | custom-call | tf_op jit(solution)/shard_map/pallas_call | solution.py:292
  7.8 0.7 %copy.8 = bf16[96,1024]{1,0:T(8,128)(2,1)} copy(bf16[96,1024]{1,0:T(8,128)(2,1)S(1)} %shard_map.64) | data formatting | bytes 393216

commit v4 on v3

--- a/solution.py
+++ b/solution.py
@@ -117,6 +117,13 @@
         pick.astype(jnp.bfloat16), lat_buf[...], preferred_element_type=jnp.float32
     ).astype(jnp.bfloat16)
 
+    def keep(step):
+        @pl.when(mine_l + step == mine_q)
+        def _():
+            window[back - step] = stage[...]
+
+    each(slots, keep)
+
     last = jnp.minimum(blocks - 1, mine_l + back)
     own = ((mine_q >= mine_l) & (mine_q <= last)).astype(jnp.int32)
     partners = last - mine_l + 1 - own
@@ -142,10 +149,6 @@
         @pl.when((target < blocks) & (target != mine_q))
         def _():
             copy_to(step).start()
-
-        @pl.when(target == mine_q)
-        def _():
-            window[back - step] = stage[...]
 
     each(slots, send)
 
@@ -248,11 +251,10 @@
         loads[5].wait()
         for slot in reversed(range(slots)):
             arrive(slot)
-            if slot == 1:
-                each(slots, drain)
         rebuild(0, slots)
         for g in range(kv):
             write(g, attend(g, 0, slots, mask, None, None)[1])
+        each(slots, drain)
     else:
         row_max[...] = jnp.full(row_max.shape, NEG, jnp.float32)
         total[...] = jnp.zeros(total.shape, jnp.float32)

time: 8.66 us -> 8.66 us (level)
  no operation moved by 1% of the time
where the time goes in v4:
time: 8.66 us; the launch traced here: 8.51 us
  Pallas kernels  7.83 us (90%)
  local copies, waits for them, and re-layouts  0.68 us (8%)
    pallas_call x1, Pallas kernels, shards(): pl.pallas_call(functools.partial(kernel, plan), out_shape=pltpu.VMEM(quer...  7.83 us
    unnamed x1, local copies, waits for them, and re-layouts  0.68 us

profile of v4, /device:TPU:11, one launch (start us, length us, event | category | flops | bytes accessed | tf_op | source)
XLA Modules:
  0.0 8.5 jit_solution(2424498343587940383)
XLA Ops:
  0.0 7.8 %shard_map.64 = bf16[96,1024]{1,0:T(8,128)(2,1)S(1)} custom-call(bf16[96,1024]{1,0:T(8,128)(2,1)} %q_hbm.1, bf16[192,128]{1,0:T(8,128)(2,1)} %bitcast.2, bf16[2,64,128]{2,1,0:T(8,128)(2,1)} %key_up_hbm.1, bf16[2,64,128]{2,1,0:T(8,128)(2,1)} %value_up_hbm.1, s32[6,128]{1,0:T(8,128)} %bitcast.3, f32[208,128]{1,0:T(8,128)} %constant.2.clone.table_hbm), custom_call_target="tpu_custom_call" | custom-call | tf_op jit(solution)/shard_map/pallas_call | solution.py:294
  7.8 0.7 %copy.8 = bf16[96,1024]{1,0:T(8,128)(2,1)} copy(bf16[96,1024]{1,0:T(8,128)(2,1)S(1)} %shard_map.64) | data formatting | bytes 393216

commit v5 on v4

--- a/solution.py
+++ b/solution.py
@@ -233,6 +233,19 @@
             part = part + sums * jnp.exp2((before - top) * factor)
         return top, part
 
+    def attend_t(g):
+        heads = range(g * group, (g + 1) * group)
+        stacked = jnp.concatenate([q_buf[:, h * width : (h + 1) * width] for h in heads])
+        scores = lax.dot_general(
+            keys[g], stacked, (((1,), (1,)), ((), ())), preferred_element_type=jnp.float32
+        )
+        scores = scores + mask_t
+        top = jnp.max(scores, axis=0, keepdims=True)
+        weights = jnp.exp2((scores - top) * factor).astype(jnp.bfloat16)
+        return lax.dot_general(
+            weights, values[g], (((0,), (0,)), ((), ())), preferred_element_type=jnp.float32
+        )
+
     def write(g, part):
         ratio = (part[:, :width] / part[:, width:]).astype(jnp.bfloat16)
         for i in range(group):
@@ -247,13 +260,25 @@
             copy_to(step).wait_send()
 
     if slots <= 8:
-        mask = bias_of(0, slots)
+        key_col = (mine_q - back) * rows + lax.broadcasted_iota(jnp.int32, (slots * rows, 1), 0)
+        key_col = key_col.astype(jnp.float32)
+        q_lane = lax.broadcasted_iota(jnp.int32, (1, group * rows), 1)
+        turn = q_lane
+        for i in range(1, group):
+            turn = jnp.where(q_lane >= i * rows, q_lane - i * rows, turn)
+        turn = (mine_q * rows + turn).astype(jnp.float32)
+        begin_t = jnp.zeros((1, group * rows), jnp.float32)
+        for doc in range(3):
+            cut = jnp.sum(jnp.where(docs <= doc, 1.0, 0.0), axis=0, keepdims=True)
+            cut = jnp.sum(cut, axis=1, keepdims=True)
+            begin_t = jnp.maximum(begin_t, jnp.where(cut <= turn, cut, 0.0))
+        mask_t = jnp.where((key_col >= begin_t) & (key_col <= turn), 0.0, NEG)
         loads[5].wait()
         for slot in reversed(range(slots)):
             arrive(slot)
         rebuild(0, slots)
         for g in range(kv):
-            write(g, attend(g, 0, slots, mask, None, None)[1])
+            write(g, attend_t(g))
         each(slots, drain)
     else:
         row_max[...] = jnp.full(row_max.shape, NEG, jnp.float32)

time: 8.66 us -> 8.64 us (level)
  no operation moved by 1% of the time
where the time goes in v5:
time: 8.64 us; the launch traced here: 8.5 us
  Pallas kernels  7.81 us (90%)
  local copies, waits for them, and re-layouts  0.68 us (8%)
    pallas_call x1, Pallas kernels, shards(): pl.pallas_call(functools.partial(kernel, plan), out_shape=pltpu.VMEM(quer...  7.81 us
    unnamed x1, local copies, waits for them, and re-layouts  0.68 us

profile of v5, /device:TPU:11, one launch (start us, length us, event | category | flops | bytes accessed | tf_op | source)
XLA Modules:
  0.0 8.5 jit_solution(12190299688174057481)
XLA Ops:
  0.0 7.8 %shard_map.64 = bf16[96,1024]{1,0:T(8,128)(2,1)S(1)} custom-call(bf16[96,1024]{1,0:T(8,128)(2,1)} %q_hbm.1, bf16[192,128]{1,0:T(8,128)(2,1)} %bitcast.2, bf16[2,64,128]{2,1,0:T(8,128)(2,1)} %key_up_hbm.1, bf16[2,64,128]{2,1,0:T(8,128)(2,1)} %value_up_hbm.1, s32[6,128]{1,0:T(8,128)} %bitcast.3, f32[208,128]{1,0:T(8,128)} %constant.2.clone.table_hbm), custom_call_target="tpu_custom_call" | custom-call | tf_op jit(solution)/shard_map/pallas_call | solution.py:319
  7.8 0.7 %copy.8 = bf16[96,1024]{1,0:T(8,128)(2,1)} copy(bf16[96,1024]{1,0:T(8,128)(2,1)S(1)} %shard_map.64) | data formatting | bytes 393216

commit v6 on v5

--- a/solution.py
+++ b/solution.py
@@ -233,13 +233,19 @@
             part = part + sums * jnp.exp2((before - top) * factor)
         return top, part
 
-    def attend_t(g):
+    def score_t(g, first, count, mask_t):
         heads = range(g * group, (g + 1) * group)
         stacked = jnp.concatenate([q_buf[:, h * width : (h + 1) * width] for h in heads])
+        at, reach = first * rows, count * rows
         scores = lax.dot_general(
-            keys[g], stacked, (((1,), (1,)), ((), ())), preferred_element_type=jnp.float32
+            keys[g, at : at + reach],
+            stacked,
+            (((1,), (1,)), ((), ())),
+            preferred_element_type=jnp.float32,
         )
-        scores = scores + mask_t
+        return scores + mask_t[at : at + reach]
+
+    def attend_t(g, scores):
         top = jnp.max(scores, axis=0, keepdims=True)
         weights = jnp.exp2((scores - top) * factor).astype(jnp.bfloat16)
         return lax.dot_general(
@@ -274,11 +280,14 @@
             begin_t = jnp.maximum(begin_t, jnp.where(cut <= turn, cut, 0.0))
         mask_t = jnp.where((key_col >= begin_t) & (key_col <= turn), 0.0, NEG)
         loads[5].wait()
-        for slot in reversed(range(slots)):
+        for slot in reversed(range(1, slots)):
             arrive(slot)
-        rebuild(0, slots)
+        rebuild(1, slots - 1)
+        nearer = [score_t(g, 1, slots - 1, mask_t) for g in range(kv)]
+        arrive(0)
+        rebuild(0, 1)
         for g in range(kv):
-            write(g, attend_t(g))
+            write(g, attend_t(g, jnp.concatenate([score_t(g, 0, 1, mask_t), nearer[g]])))
         each(slots, drain)
     else:
         row_max[...] = jnp.full(row_max.shape, NEG, jnp.float32)

time: 8.64 us -> 8.97 us (1.038)
  Pallas kernels: 7.81 us -> 8.14 us
    pallas_call x1, Pallas kernels: 7.81 us -> 8.14 us  [shards(): pl.pallas_call(functools.partial(kernel, plan), out_shape=pltpu.VMEM(quer...]
where the time goes in v6:
time: 8.97 us; the launch traced here: 8.83 us
  Pallas kernels  8.14 us (91%)
  local copies, waits for them, and re-layouts  0.68 us (8%)
    pallas_call x1, Pallas kernels, shards(): pl.pallas_call(functools.partial(kernel, plan), out_shape=pltpu.VMEM(quer...  8.14 us
    unnamed x1, local copies, waits for them, and re-layouts  0.68 us

profile of v6, /device:TPU:11, one launch (start us, length us, event | category | flops | bytes accessed | tf_op | source)
XLA Modules:
  0.0 8.8 jit_solution(9905852482747685520)
XLA Ops:
  0.0 8.1 %shard_map.64 = bf16[96,1024]{1,0:T(8,128)(2,1)S(1)} custom-call(bf16[96,1024]{1,0:T(8,128)(2,1)} %q_hbm.1, bf16[192,128]{1,0:T(8,128)(2,1)} %bitcast.2, bf16[2,64,128]{2,1,0:T(8,128)(2,1)} %key_up_hbm.1, bf16[2,64,128]{2,1,0:T(8,128)(2,1)} %value_up_hbm.1, s32[6,128]{1,0:T(8,128)} %bitcast.3, f32[208,128]{1,0:T(8,128)} %constant.2.clone.table_hbm), custom_call_target="tpu_custom_call" | custom-call | tf_op jit(solution)/shard_map/pallas_call | solution.py:328
  8.1 0.7 %copy.8 = bf16[96,1024]{1,0:T(8,128)(2,1)} copy(bf16[96,1024]{1,0:T(8,128)(2,1)S(1)} %shard_map.64) | data formatting | bytes 393216
